TPU v7x, 32 devices: a whole 2x2x4 slice. The times are simulated.
32 devices in a mesh: doc: 8 (over z, x), fsdp: 4 (over y, core).
Axes of the slice: x: 2, y: 2, z: 4, core: 2. Of those that a mesh axis runs over, the one named last changes fastest.
Arguments:
- activations: bfloat16 [128, 256, 8192], P('doc', None, 'fsdp'), may hold values from -6 to 6
- cotangents: bfloat16 [128, 256, 8192], P('doc', None, 'fsdp'), may hold values from -6 to 6
- adapter_down_matrix: bfloat16 [8192, 128], P('fsdp'), may hold values from -0.0625 to 0.0625
- targets: bfloat16 [512, 2048], P('fsdp', 'doc'), may hold values from -0.125 to 0.125
- projection_sign_seed: int32 [1], replicated, may hold values from 0 to 999999
Outputs:
- feature_gram: float32 [2048, 2048], P('doc', 'fsdp')
- scores: float32 [128, 512], P('doc', 'fsdp')
All inputs are finite; a program needn't handle non-finite values.
Results may differ from a plain program's by a relative error of at most 0.025.
Values may be sent and summed in bfloat16 or wider, within the bound.
A program may use at most 128 MiB of HBM per device.

v0:
```python
import math

import jax
import jax.numpy as jnp
from jax import lax
from jax.sharding import PartitionSpec as P

PROJECTED_DIMS = 2048


norm_eps = 1e-06


def sign_table(param_ids, column_ids, seed_value):
    hashed = param_ids[:, None] * -1640531535 + column_ids[None, :] * 668265263 + seed_value
    hashed = hashed ^ hashed >> 15 & 131071
    hashed = hashed * -2048144789
    hashed = hashed ^ hashed >> 13 & 524287
    hashed = hashed * -1028477387
    hashed = hashed ^ hashed >> 16 & 65535
    low_bit = hashed >> 7 & 1
    return (1 - 2 * low_bit).astype(jnp.bfloat16)


def body(activations, cotangents, adapter_down_matrix, targets, projection_sign_seed):
    document_count = lax.axis_size("doc")
    shard_count = lax.axis_size("fsdp")
    doc_index = lax.axis_index("doc")
    shard_index = lax.axis_index("fsdp")
    resident_documents, sequence_length, resident_width = activations.shape
    adapter_rank = adapter_down_matrix.shape[1]
    complete_width = resident_width * shard_count
    document_total = resident_documents * document_count
    gradient_scale = 1.0 / math.sqrt(adapter_rank * complete_width * sequence_length)
    seed_value = projection_sign_seed[0]
    flattened_tokens = activations.reshape(resident_documents * sequence_length, resident_width)
    partial_reduced = jnp.dot(
        flattened_tokens, adapter_down_matrix, preferred_element_type=jnp.float32
    )
    reduced_rank_rows = lax.psum(partial_reduced, "fsdp")
    reduced_rank_rows = reduced_rank_rows.astype(jnp.bfloat16).reshape(
        resident_documents, sequence_length, adapter_rank
    )
    document_gradients = jnp.einsum(
        "esr,esc->erc", reduced_rank_rows, cotangents, preferred_element_type=jnp.float32
    )
    flattened_gradients = document_gradients.astype(jnp.bfloat16).reshape(
        resident_documents, adapter_rank * resident_width
    )
    piece_length = adapter_rank * resident_width // document_count
    local_ids = doc_index * piece_length + jnp.arange(piece_length, dtype=jnp.int32)
    sign_rows = sign_table(
        local_ids // resident_width * complete_width
        + shard_index * resident_width
        + local_ids % resident_width,
        jnp.arange(PROJECTED_DIMS, dtype=jnp.int32),
        seed_value,
    )
    exchanged = lax.all_to_all(flattened_gradients, "doc", split_axis=1, concat_axis=0, tiled=True)
    feature_part = lax.psum_scatter(
        lax.dot_general(
            sign_rows, exchanged, (((0,), (1,)), ((), ())), preferred_element_type=jnp.float32
        ),
        ("doc", "fsdp"),
        scatter_dimension=0,
        tiled=True,
    )
    feature_part = (feature_part * gradient_scale).astype(jnp.bfloat16)
    features_t = lax.all_gather(feature_part, ("doc", "fsdp"), axis=0, tiled=True)
    rows_len = PROJECTED_DIMS // document_count
    cols_len = PROJECTED_DIMS // shard_count
    gram_rows = lax.dynamic_slice_in_dim(features_t, doc_index * rows_len, rows_len, 0)
    gram_cols = lax.dynamic_slice_in_dim(features_t, shard_index * cols_len, cols_len, 0)
    feature_gram = (
        lax.dot_general(
            gram_rows, gram_cols, (((1,), (1,)), ((), ())), preferred_element_type=jnp.float32
        )
        / document_total
    )
    partial_scores = lax.dot_general(
        gram_rows, targets, (((0,), (1,)), ((), ())), preferred_element_type=jnp.float32
    )
    squares = jnp.sum(jnp.square(gram_rows.astype(jnp.float32)), axis=0)
    raw_scores, energy = (
        lax.psum_scatter(
            partial_scores.astype(jnp.bfloat16), "doc", scatter_dimension=0, tiled=True
        ).astype(jnp.float32),
        lax.psum_scatter(
            squares.astype(jnp.bfloat16), "doc", scatter_dimension=0, tiled=True
        ).astype(jnp.float32),
    )
    inverse_rms = lax.rsqrt(energy / PROJECTED_DIMS + norm_eps)
    scores = raw_scores * inverse_rms[:, None]
    return (feature_gram, scores)


def solution(mesh):
    in_specs = (
        P("doc", None, "fsdp"),
        P("doc", None, "fsdp"),
        P("fsdp", None),
        P("fsdp", "doc"),
        P(),
    )
    out_specs = (P("doc", "fsdp"), P("doc", "fsdp"))
    return jax.shard_map(body, mesh=mesh, in_specs=in_specs, out_specs=out_specs, check_vma=False)
```

profile of v0, /device:TPU:1, one launch (start us, length us, event | category | flops | bytes accessed | tf_op | source)
XLA Modules:
  0.0 661.4 jit_solution(5231703186044070535)
XLA Ops:
  7.2 1.0 copy-done
  8.2 9.5 %fusion.29 = f32[4096,128]{1,0:T(8,128)} fusion(bf16[4096,2048]{1,0:T(8,128)(2,1)} %bitcast.16, bf16[2048,128]{1,0:T(8,128)(2,1)S(1)} %copy-done), kind=kOutput, calls=%fused_computation.45 | convolution fusion | flops 2147483648 | bytes 19398656 | tf_op jit(solution)/shard_map/dot_general | solution.py:37
  17.7 43.6 %all-reduce.2 = bf16[4096,128]{1,0:T(8,128)(2,1)S(1)} all-reduce(f32[4096,128]{1,0:T(8,128)} %fusion.29), channel_id=1, replica_groups=mesh['doc'=8,'fsdp'=4] {'fsdp'}, use_global_device_ids=true, to_apply=%region_0.0 | all-reduce | flops 524288 | bytes 3145728 | tf_op jit(solution)/shard_map/psum | solution.py:40
  61.3 11.4 %convolution_convert_fusion = bf16[16,128,2048]{2,1,0:T(8,128)(2,1)} fusion(bf16[16,256,128]{2,1,0:T(8,128)(2,1)S(1)} %bitcast.15, bf16[16,256,2048]{2,1,0:T(8,128)(2,1)} %param.6), kind=kOutput, calls=%fused_computation.2 | convolution fusion | flops 2151677952 | bytes 26214400 | tf_op jit(solution)/shard_map/esr,esc->erc/dot_general | solution.py:44
  72.7 13.5 %all_to_all.14 = bf16[16,8,32768]{2,1,0:T(8,128)(2,1)} reshape(bf16[16,128,2048]{2,1,0:T(8,128)(2,1)} %convolution_convert_fusion) | data formatting | bytes 16777216 | tf_op jit(solution)/shard_map/all_to_all | solution.py:59
  86.2 11.2 %copy.11 = bf16[16,8,32768]{2,0,1:T(8,128)(2,1)} copy(bf16[16,8,32768]{2,1,0:T(8,128)(2,1)} %all_to_all.14) | data formatting | bytes 16777216 | tf_op jit(solution)/shard_map/all_to_all | solution.py:59
  97.4 5.5 all-to-all-start
  103.0 0.2 reduce-scatter.3.cloned.1.call-start
  103.8 0.1 fusion.4
  104.0 181.8 %all-to-all-done = bf16[16,8,32768]{2,0,1:T(8,128)(2,1)} async-done(((bf16[16,8,32768]{2,0,1:T(8,128)(2,1)}), bf16[16,8,32768]{2,0,1:T(8,128)(2,1)}, u32[]{:S(2)}, u32[]{:S(2)}) %all-to-all-start) | async-done | bytes 8388640 | tf_op jit(solution)/shard_map/all_to_all | solution.py:59
  285.8 144.0 %fusion = f32[2048,128]{1,0:T(8,128)} fusion(bf16[128,32768]{1,0:T(8,128)(2,1)} %bitcast.4, s32[]{:T(128)} %bitcast.14, s32[2048]{0:T(1024)S(1)} %iota_multiply_fusion, s32[32768]{0:T(1024)S(1)} %fusion.4), kind=kOutput, calls=%fused_computation.1 | convolution fusion | flops 18387828736 | bytes 9576452 | tf_op jit(solution)/shard_map/dot_general | solution.py:61
  429.8 0.0 reduce-scatter.3.cloned.1.call-update
  429.9 0.0 reduce-scatter.5.cloned.1.call-start
  429.9 0.6 dynamic-slice
  431.2 127.1 %reduce-scatter.3.cloned.1.call-done = f32[64,128]{1,0:T(8,128)} async-done(((f32[2048,128]{1,0:T(8,128)}), f32[64,128]{1,0:T(8,128)}) %reduce-scatter.3.cloned.1.call-update) | async-done | bytes 32784 | tf_op jit(solution)/shard_map/reduce_scatter | solution.py:60
  558.2 0.8 multiply_convert_fusion
  559.0 43.6 %all_gather.3 = bf16[2048,128]{1,0:T(8,128)(2,1)S(1)} all-gather(bf16[64,128]{1,0:T(8,128)(2,1)S(1)} %multiply_convert_fusion), channel_id=1, replica_groups=mesh['doc'=8,'fsdp'=4] {'doc','fsdp'}, dimensions={0}, use_global_device_ids=true | all-gather | bytes 540672 | tf_op jit(solution)/shard_map/all_gather | solution.py:69
  602.6 0.1 multiply_reduce_fusion
  602.7 1.0 convolution_multiply_fusion
  603.7 0.8 convolution_convert_fusion.1
  604.5 13.7 %all-reduce = bf16[128]{0:T(256)(128)(2,1)S(1)} all-reduce(bf16[128]{0:T(256)(128)(2,1)S(1)} %multiply_reduce_fusion), channel_id=4, replica_groups=mesh['doc'=8,'fsdp'=4] {'doc'}, use_global_device_ids=true, to_apply=%region_4.5.clone | all-reduce | flops 128 | bytes 512
  618.2 0.1 fusion.17
  618.3 35.0 %reduce-scatter.5.cloned.1.call-done = bf16[16,128]{1,0:T(8,128)(2,1)} async-done(((bf16[128,128]{1,0:T(8,128)(2,1)}), bf16[16,128]{1,0:T(8,128)(2,1)}) %reduce-scatter.5.cloned.1.call-update) | async-done | bytes 4112 | tf_op jit(solution)/shard_map/reduce_scatter | solution.py:85
  653.3 1.3 convert_multiply_fusion
  (9 shorter events, 0.0 us)
Async XLA Ops:
  7.2 1.1 copy-start
  97.4 188.4 %all-to-all-start = ((bf16[16,8,32768]{2,0,1:T(8,128)(2,1)}), bf16[16,8,32768]{2,0,1:T(8,128)(2,1)}, u32[]{:S(2)}, u32[]{:S(2)}) async-start(bf16[16,8,32768]{2,0,1:T(8,128)(2,1)} %copy.11), calls=%async_computation | async-start | bytes 16777216 | tf_op jit(solution)/shard_map/all_to_all | solution.py:59
  103.0 455.3 %reduce-scatter.3.cloned.1.call-start = ((), (), s32[]{:S(2)}) async-start(), calls=%async_computation.3 | async-start | bytes 1081344 | tf_op jit(solution)/shard_map/reduce_scatter | solution.py:60
  285.8 144.1 %copy-start.3 = (u32[32]{0:T(128)S(1)}, u32[32]{0:T(128)}, u32[]{:S(2)}) copy-start(u32[32]{0:T(128)} %constant.85) | copy-start | bytes 388
  285.8 317.9 %copy-start.2 = (bf16[128,256]{1,0:T(8,128)(2,1)S(1)}, bf16[128,256]{1,0:T(8,128)(2,1)}, u32[]{:S(2)}) copy-start(bf16[128,256]{1,0:T(8,128)(2,1)} %param.8) | copy-start | bytes 196612
  285.8 368.8 %copy-start.1 = (bf16[2048,128]{1,0:T(8,128)(2,1)S(1)}, bf16[2048,128]{1,0:T(8,128)(2,1)}, u32[]{:S(2)}) copy-start(bf16[2048,128]{1,0:T(8,128)(2,1)} %param.7) | copy-start | bytes 1572868
  429.9 223.4 %reduce-scatter.5.cloned.1.call-start = ((), (), s32[]{:S(2)}) async-start(), calls=%async_computation.4 | async-start | bytes 36864 | tf_op jit(solution)/shard_map/reduce_scatter | solution.py:85
Sparse Core Ops, SparseCore 0:
  430.0 128.2 reduce-scatter.2
  604.6 48.5 reduce-scatter.4
where the time goes:
time: 665 us; the launch traced here: 661 us
  waiting for transfers between devices  344 us (52%)
  matrix products  167 us (25%)
  blocking collectives  101 us (15%)
  local copies, waits for them, and re-layouts  26.3 us (4%)
  between operations  15.4 us (2%)
    all_to_all x1, waiting for transfers between devices, body(): lax.all_to_all(flattened_gradients, 'doc', split_axis=1, concat_axis=0, t...  182 us
    dot_general x1, matrix products, body(): lax.dot_general(sign_rows, exchanged, (((0,), (1,)), ((), ())), preferred...  144 us
    reduce_scatter x1, waiting for transfers between devices, body(): lax.psum_scatter(lax.dot_general(sign_rows, exchanged, (((0,), (1,)), (()...  127 us
    psum x1, blocking collectives, body(): reduced_rank_rows = lax.psum(partial_reduced, 'fsdp')  43.6 us
    all_gather x1, blocking collectives, body(): lax.all_gather(feature_part, ('doc', 'fsdp'), axis=0, tiled=True)  43.6 us
    reduce_scatter x1, waiting for transfers between devices, body(): lax.psum_scatter(partial_scores.astype(jnp.bfloat16), 'doc', scatter_dime...  35 us
    all_to_all x2, local copies, waits for them, and re-layouts, body(): lax.all_to_all(flattened_gradients, 'doc', split_axis=1, concat_axis=0, t...  24.7 us
    unnamed x1, blocking collectives  13.7 us
  transfers between devices with their start and end apart: 3, of which 3 were waited for; matrix products, arithmetic and copies ran while one was open for 0% of the time, Pallas kernels for 0%

commit v1 on v0

v1 whole, which is shorter than its diff:
```python
import functools
import math

import jax
import jax.numpy as jnp
from jax import lax
from jax.experimental import pallas as pl
from jax.experimental.pallas import tpu as pltpu
from jax.sharding import PartitionSpec as P

PROJECTED_DIMS = 2048
MESH = pl.DeviceIdType.MESH
norm_eps = 1e-06
ROWS = 32
AHEAD = 4


def wrap(value):
    return jnp.int32((value + 2**31) % 2**32 - 2**31)


def signs(hashed):
    hashed = hashed ^ lax.shift_right_logical(hashed, 15)
    hashed = hashed * wrap(-2048144789)
    hashed = hashed ^ lax.shift_right_logical(hashed, 13)
    hashed = hashed * wrap(-1028477387 * 256)
    hashed = hashed ^ (hashed << 16)
    return jnp.where(hashed < 0, jnp.bfloat16(-1), jnp.bfloat16(1))


def greet(groups):
    barrier = pltpu.get_barrier_semaphore()
    count = 0
    for axis, size in groups:
        me = lax.axis_index(axis)
        for k in range(1, size):
            pl.semaphore_signal(
                barrier, inc=1, device_id={axis: lax.rem(me + k, size)}, device_id_type=MESH
            )
            count += 1
    pl.semaphore_wait(barrier, count)


def exchange(axis, size, source, target, send, recv):
    me = lax.axis_index(axis)
    copies = []
    for k in range(1, size):
        peer = lax.rem(me + k, size)
        copies.append(
            pltpu.make_async_remote_copy(
                src_ref=source(peer),
                dst_ref=target(me),
                send_sem=send.at[k],
                recv_sem=recv.at[k],
                device_id={axis: peer},
                device_id_type=MESH,
            )
        )
    return copies


def run(copies):
    for copy in copies:
        copy.start()
    for copy in copies:
        copy.wait()


def rank_kernel(shards, part_ref, out_ref, got, s0, r0, s1, r1):
    me = lax.axis_index("fsdp")
    rows = part_ref.shape[0] // shards

    def block(i):
        return pl.ds(pl.multiple_of(i * rows, rows), rows)

    greet([("fsdp", shards)])
    run(exchange("fsdp", shards, lambda p: part_ref.at[block(p)], lambda m: got.at[m], s0, r0))
    total = part_ref[block(me), :].astype(jnp.float32)
    for k in range(1, shards):
        total += got[lax.rem(me + k, shards)].astype(jnp.float32)
    out_ref[block(me), :] = total.astype(jnp.bfloat16)
    run(exchange("fsdp", shards, lambda p: out_ref.at[block(me)], lambda m: out_ref.at[block(m)], s1, r1))


def project_kernel(
    nd, nf, scale, seed_ref, grads_ref, tin_ref, gram_ref, scores_ref,
    landed, base, total, targets, outgoing, got_a, mid, got_b, feats,
    gs, gr, own_sem, ts, tr, s0, r0, s1, r1, s2, r2, s3, r3,
):
    doc, shard = lax.axis_index("doc"), lax.axis_index("fsdp")
    ranks, docs, width = grads_ref.shape
    steps = ranks // nd
    complete_width = width * nf
    rows_len, cols_len = PROJECTED_DIMS // nd, PROJECTED_DIMS // nf
    everyone = docs * nd
    kp = min(512, width)
    kc = 512

    def doc_rows(i):
        return pl.ds(pl.multiple_of(i * docs, docs), docs)

    def target_cols(i):
        return pl.ds(pl.multiple_of(i * rows_len, rows_len), rows_len)

    def grad_copy(s, k):
        peer = lax.rem(doc + k, nd)
        return pltpu.make_async_remote_copy(
            src_ref=grads_ref.at[peer * steps + s],
            dst_ref=landed.at[s, doc_rows(doc)],
            send_sem=gs.at[s, k],
            recv_sem=gr.at[s, k],
            device_id={"doc": peer},
            device_id_type=MESH,
        )

    def own_copy(s):
        return pltpu.make_async_copy(
            grads_ref.at[doc * steps + s], landed.at[s, doc_rows(doc)], own_sem.at[s]
        )

    def send(s, carry):
        def one(k, c):
            grad_copy(s, k).start()
            return c

        lax.fori_loop(1, nd, one, 0)
        own_copy(s).start()
        return carry

    greet([("doc", nd), ("fsdp", nf)])
    ahead = min(AHEAD, steps)
    lax.fori_loop(0, ahead, send, 0)
    target_copies = exchange("doc", nd, lambda p: tin_ref, lambda m: targets.at[:, target_cols(m)], ts, tr)
    for copy in target_copies:
        copy.start()
    targets[:, target_cols(doc)] = tin_ref[...]

    column = lax.broadcasted_iota(jnp.int32, base.shape, 1)
    row = lax.broadcasted_iota(jnp.int32, base.shape, 0)
    base[...] = row * wrap(-1640531535) + column * wrap(668265263) + seed_ref[0]
    total[...] = jnp.zeros_like(total)

    def project(s, carry):
        @pl.when(s + ahead < steps)
        def _():
            send(s + ahead, 0)

        def one(k, c):
            grad_copy(s, k).wait()
            return c

        lax.fori_loop(1, nd, one, 0)
        own_copy(s).wait()

        def chunk(j, c):
            first = (doc * steps + s) * complete_width + shard * width + j * kp
            offset = first * wrap(-1640531535)
            left = landed[s, :, pl.ds(pl.multiple_of(j * kp, kp), kp)]
            for c0 in range(0, PROJECTED_DIMS, kc):
                held = base[:, c0 : c0 + kc] + offset
                table = jnp.concatenate(
                    [signs(held + wrap(q * ROWS * -1640531535)) for q in range(kp // ROWS)], 0
                )
                total[:, c0 : c0 + kc] += jnp.dot(left, table, preferred_element_type=jnp.float32)
            return c

        return lax.fori_loop(0, width // kp, chunk, carry)

    lax.fori_loop(0, steps, project, 0)

    for f in range(nf):
        outgoing[f] = total[:, f * cols_len : (f + 1) * cols_len].astype(jnp.bfloat16)
    run(exchange("fsdp", nf, lambda p: outgoing.at[p], lambda m: got_a.at[m], s0, r0))
    part = outgoing[shard].astype(jnp.float32)
    for k in range(1, nf):
        part += got_a[lax.rem(shard + k, nf)].astype(jnp.float32)
    mid[...] = part.astype(jnp.bfloat16)
    run(exchange("doc", nd, lambda p: mid.at[doc_rows(p)], lambda m: got_b.at[m], s1, r1))
    feature = mid[doc_rows(doc), :].astype(jnp.float32)
    for k in range(1, nd):
        feature += got_b[lax.rem(doc + k, nd)].astype(jnp.float32)
    feats[shard, doc_rows(doc), :] = (feature * scale).astype(jnp.bfloat16)
    run(
        exchange(
            "doc", nd, lambda p: feats.at[shard, doc_rows(doc)],
            lambda m: feats.at[shard, doc_rows(m)], s2, r2,
        )
    )
    run(exchange("fsdp", nf, lambda p: feats.at[shard], lambda m: feats.at[m], s3, r3))
    for copy in target_copies:
        copy.wait()

    per = cols_len // rows_len
    gram_rows = feats[doc // per, :, pl.ds(pl.multiple_of(doc % per * rows_len, rows_len), rows_len)]
    gram_ref[...] = lax.dot_general(
        gram_rows, feats[shard], (((0,), (0,)), ((), ())), preferred_element_type=jnp.float32
    ) / everyone
    raw = jnp.zeros(scores_ref.shape, jnp.float32)
    energy = jnp.zeros((docs, 1), jnp.float32)
    for f in range(nf):
        mine = feats[f, doc_rows(doc), :]
        raw += lax.dot_general(
            mine, targets[:, f * cols_len : (f + 1) * cols_len],
            (((1,), (1,)), ((), ())), preferred_element_type=jnp.float32,
        )
        energy += jnp.sum(jnp.square(mine.astype(jnp.float32)), axis=1, keepdims=True)
    scores_ref[...] = raw * lax.rsqrt(energy / PROJECTED_DIMS + norm_eps)


def body(activations, cotangents, adapter_down_matrix, targets, projection_sign_seed):
    nd, nf = lax.axis_size("doc"), lax.axis_size("fsdp")
    docs, tokens, width = activations.shape
    rank = adapter_down_matrix.shape[1]
    scale = 1.0 / math.sqrt(rank * width * nf * tokens)
    steps = rank // nd
    rows_len, cols_len = PROJECTED_DIMS // nd, PROJECTED_DIMS // nf
    vmem = pl.BlockSpec(memory_space=pltpu.VMEM)
    bf16, f32 = jnp.bfloat16, jnp.float32
    dma = pltpu.SemaphoreType.DMA

    part = jnp.dot(
        activations.reshape(docs * tokens, width), adapter_down_matrix, preferred_element_type=f32
    ).astype(bf16)
    low = pl.pallas_call(
        functools.partial(rank_kernel, nf),
        out_shape=jax.ShapeDtypeStruct((docs * tokens, rank), bf16),
        in_specs=[vmem],
        out_specs=vmem,
        scratch_shapes=[pltpu.VMEM((nf, docs * tokens // nf, rank), bf16)] + [dma((nf,))] * 4,
        compiler_params=pltpu.CompilerParams(
            collective_id=0, has_side_effects=True, vmem_limit_bytes=32 * 2**20
        ),
    )(part)
    grads = jnp.einsum(
        "esr,esc->rec", low.reshape(docs, tokens, rank), cotangents, preferred_element_type=f32
    ).astype(bf16)
    return pl.pallas_call(
        functools.partial(project_kernel, nd, nf, scale),
        out_shape=(
            jax.ShapeDtypeStruct((rows_len, cols_len), f32),
            jax.ShapeDtypeStruct((docs, targets.shape[0]), f32),
        ),
        in_specs=[
            pl.BlockSpec(memory_space=pltpu.SMEM), pl.BlockSpec(memory_space=pl.ANY), vmem,
        ],
        out_specs=(vmem, vmem),
        scratch_shapes=[
            pltpu.VMEM((steps, docs * nd, width), bf16),
            pltpu.VMEM((ROWS, PROJECTED_DIMS), jnp.int32),
            pltpu.VMEM((docs * nd, PROJECTED_DIMS), f32),
            pltpu.VMEM((targets.shape[0], PROJECTED_DIMS), bf16),
            pltpu.VMEM((nf, docs * nd, cols_len), bf16),
            pltpu.VMEM((nf, docs * nd, cols_len), bf16),
            pltpu.VMEM((docs * nd, cols_len), bf16),
            pltpu.VMEM((nd, docs, cols_len), bf16),
            pltpu.VMEM((nf, docs * nd, cols_len), bf16),
            dma((steps, nd)), dma((steps, nd)), dma((steps,)),
            dma((nd,)), dma((nd,)), dma((nf,)), dma((nf,)),
            dma((nd,)), dma((nd,)), dma((nd,)), dma((nd,)), dma((nf,)), dma((nf,)),
        ],
        compiler_params=pltpu.CompilerParams(
            collective_id=1, has_side_effects=True, vmem_limit_bytes=56 * 2**20
        ),
    )(projection_sign_seed, grads, targets)


def solution(mesh):
    in_specs = (
        P("doc", None, "fsdp"),
        P("doc", None, "fsdp"),
        P("fsdp", None),
        P("fsdp", "doc"),
        P(),
    )
    out_specs = (P("doc", "fsdp"), P("doc", "fsdp"))
    return jax.shard_map(body, mesh=mesh, in_specs=in_specs, out_specs=out_specs, check_vma=False)
```

time: 665 us -> 303 us (0.46)
  waiting for transfers between devices: 344 us -> 0 us
  Pallas kernels: 0 us -> 266 us
  matrix products: 167 us -> 19.7 us
  blocking collectives: 101 us -> 0 us
  between operations: 15.4 us -> 1.31 us
  local copies, waits for them, and re-layouts: 26.3 us -> 15.4 us
    pallas_call x0 -> x2, Pallas kernels: none -> 266 us  [the longest x1 239 us: body(): pl.pallas_call(functools.partial(project_kernel, nd, nf, scale), out_shap...]
    all_to_all x1 -> x0, waiting for transfers between devices: 182 us -> none  [body(): lax.all_to_all(flattened_gradients, 'doc', split_axis=1, concat_axis=0, t...]
    reduce_scatter x2 -> x0, waiting for transfers between devices: 162 us -> none  [the longest x1 127 us: body(): lax.psum_scatter(lax.dot_general(sign_rows, exchanged, (((0,), (1,)), (()...]
    dot_general x5 -> x2, matrix products: 167 us -> 19.7 us  [the longest x1 11.4 us: body(): jnp.einsum('esr,esc->rec', low.reshape(docs, tokens, rank), cotangents, p...]
    psum x1 -> x0, blocking collectives: 43.6 us -> none  [body(): reduced_rank_rows = lax.psum(partial_reduced, 'fsdp')]
    all_gather x1 -> x0, blocking collectives: 43.6 us -> none  [body(): lax.all_gather(feature_part, ('doc', 'fsdp'), axis=0, tiled=True)]
    all_to_all x2 -> x0, local copies, waits for them, and re-layouts: 24.7 us -> none  [body(): lax.all_to_all(flattened_gradients, 'doc', split_axis=1, concat_axis=0, t...]
    unnamed x1 -> x0, blocking collectives: 13.7 us -> none
  transfers between devices with their start and end apart: 3 -> 0, of which waited for: 3 -> 0; matrix products, arithmetic and copies ran while one was open for 0% -> 0% of each run, Pallas kernels for 0% -> 0%
where the time goes in v1:
time: 303 us
  Pallas kernels  266 us (88%)
  matrix products  19.7 us (7%)
  local copies, waits for them, and re-layouts  15.4 us (5%)
    pallas_call x1, Pallas kernels, body(): pl.pallas_call(functools.partial(project_kernel, nd, nf, scale), out_shap...  239 us
    pallas_call x1, Pallas kernels, body(): pl.pallas_call(functools.partial(rank_kernel, nf), out_shape=jax.ShapeDty...  27.6 us
    dot_general x1, matrix products, body(): jnp.einsum('esr,esc->rec', low.reshape(docs, tokens, rank), cotangents, p...  11.4 us
    dot_general x1, local copies, waits for them, and re-layouts, body(): jnp.einsum('esr,esc->rec', low.reshape(docs, tokens, rank), cotangents, p...  11.2 us
    dot_general x1, matrix products, body(): jnp.dot(activations.reshape(docs * tokens, width), adapter_down_matrix, p...  8.22 us

profile of v1, /device:TPU:1, one launch (start us, length us, event | category | flops | bytes accessed | tf_op | source)
XLA Modules:
  0.0 302.6 jit_solution(5048936781847049594)
XLA Ops:
  0.6 0.0 copy-start
  0.6 1.0 copy-done
  1.7 8.2 %convolution_convert_fusion.part_ref = bf16[4096,128]{1,0:T(8,128)(2,1)S(1)} fusion(bf16[4096,2048]{1,0:T(8,128)(2,1)} %bitcast.11, bf16[2048,128]{1,0:T(8,128)(2,1)S(1)} %copy-done), kind=kOutput, calls=%fused_computation.2 | convolution fusion | flops 2148007936 | bytes 18350080 | tf_op jit(solution)/shard_map/dot_general | solution.py:221
  9.9 27.6 %shard_map.68 = bf16[4096,128]{1,0:T(8,128)(2,1)S(1)} custom-call(bf16[4096,128]{1,0:T(8,128)(2,1)S(1)} %convolution_convert_fusion.part_ref), custom_call_target="tpu_custom_call" | custom-call | tf_op jit(solution)/shard_map/pallas_call | solution.py:224
  37.5 11.4 %fusion.1 = bf16[16,128,2048]{2,1,0:T(8,128)(2,1)} fusion(bf16[16,256,128]{2,1,0:T(8,128)(2,1)S(1)} %bitcast.9, bf16[16,256,2048]{2,1,0:T(8,128)(2,1)} %param.6), kind=kOutput, calls=%fused_computation.3 | convolution fusion | flops 2147483648 | bytes 26214400 | tf_op jit(solution)/shard_map/esr,esc->rec/dot_general | solution.py:234
  48.9 11.2 %copy.13 = bf16[16,128,2048]{2,0,1:T(8,128)(2,1)} copy(bf16[16,128,2048]{2,1,0:T(8,128)(2,1)} %fusion.1) | data formatting | bytes 16777216 | tf_op jit(solution)/shard_map/esr,esc->rec/dot_general | solution.py:234
  60.8 238.6 %shard_map.69 = (f32[256,512]{1,0:T(8,128)}, f32[16,128]{1,0:T(8,128)}) custom-call(s32[1]{0:T(128)S(6)} %copy.16.seed_ref, bf16[128,16,2048]{2,1,0:T(8,128)(2,1)} %bitcast.10, bf16[128,256]{1,0:T(8,128)(2,1)} %tin_ref.1), custom_call_target="tpu_custom_call" | custom-call | tf_op jit(solution)/shard_map/pallas_call | solution.py:237
  299.4 1.9 copy.17
  301.3 1.3 copy.18
Async XLA Ops:
  0.6 1.0 copy-start

commit v2 on v1

--- a/solution.py
+++ b/solution.py
@@ -13,6 +13,7 @@
 norm_eps = 1e-06
 ROWS = 32
 AHEAD = 4
+HALVED = 4
 
 
 def wrap(value):
@@ -84,12 +85,16 @@
 
 def project_kernel(
     nd, nf, scale, seed_ref, grads_ref, tin_ref, gram_ref, scores_ref,
-    landed, base, total, targets, outgoing, got_a, mid, got_b, feats,
-    gs, gr, own_sem, ts, tr, s0, r0, s1, r1, s2, r2, s3, r3,
+    landed, near, base, total, targets, outgoing, got_a, mid, got_b, feats,
+    gs, gr, own_sem, hs, hr, near_sem, ts, tr, s0, r0, s1, r1, s2, r2, s3, r3,
 ):
     doc, shard = lax.axis_index("doc"), lax.axis_index("fsdp")
     ranks, docs, width = grads_ref.shape
-    steps = ranks // nd
+    half = nd // 2
+    whole_ranks = ranks - ranks // HALVED
+    steps, near_steps = whole_ranks // nd, (ranks - whole_ranks) // half
+    side, place = doc // half, lax.rem(doc, half)
+    near_docs = docs * half
     complete_width = width * nf
     rows_len, cols_len = PROJECTED_DIMS // nd, PROJECTED_DIMS // nf
     everyone = docs * nd
@@ -127,9 +132,38 @@
         own_copy(s).start()
         return carry
 
+    def near_copy(s, k):
+        peer = lax.rem(place + k, half)
+        return pltpu.make_async_remote_copy(
+            src_ref=grads_ref.at[whole_ranks + peer * near_steps + s],
+            dst_ref=near.at[s, doc_rows(place)],
+            send_sem=hs.at[s, k],
+            recv_sem=hr.at[s, k],
+            device_id={"doc": side * half + peer},
+            device_id_type=MESH,
+        )
+
+    def near_own(s):
+        return pltpu.make_async_copy(
+            grads_ref.at[whole_ranks + place * near_steps + s],
+            near.at[s, doc_rows(place)],
+            near_sem.at[s],
+        )
+
+    def near_send(s, carry):
+        def one(k, c):
+            near_copy(s, k).start()
+            return c
+
+        lax.fori_loop(1, half, one, 0)
+        near_own(s).start()
+        return carry
+
     greet([("doc", nd), ("fsdp", nf)])
     ahead = min(AHEAD, steps)
-    lax.fori_loop(0, ahead, send, 0)
+    for i in range(ahead):
+        lax.fori_loop(near_steps * i // ahead, near_steps * (i + 1) // ahead, near_send, 0)
+        send(i, 0)
     target_copies = exchange("doc", nd, lambda p: tin_ref, lambda m: targets.at[:, target_cols(m)], ts, tr)
     for copy in target_copies:
         copy.start()
@@ -140,31 +174,54 @@
     base[...] = row * wrap(-1640531535) + column * wrap(668265263) + seed_ref[0]
     total[...] = jnp.zeros_like(total)
 
-    def project(s, carry):
-        @pl.when(s + ahead < steps)
-        def _():
-            send(s + ahead, 0)
-
-        def one(k, c):
-            grad_copy(s, k).wait()
-            return c
-
-        lax.fori_loop(1, nd, one, 0)
-        own_copy(s).wait()
-
+    def multiply(block, rank, rows):
         def chunk(j, c):
-            first = (doc * steps + s) * complete_width + shard * width + j * kp
+            first = rank * complete_width + shard * width + j * kp
             offset = first * wrap(-1640531535)
-            left = landed[s, :, pl.ds(pl.multiple_of(j * kp, kp), kp)]
+            left = block[:, pl.ds(pl.multiple_of(j * kp, kp), kp)]
             for c0 in range(0, PROJECTED_DIMS, kc):
                 held = base[:, c0 : c0 + kc] + offset
                 table = jnp.concatenate(
                     [signs(held + wrap(q * ROWS * -1640531535)) for q in range(kp // ROWS)], 0
                 )
-                total[:, c0 : c0 + kc] += jnp.dot(left, table, preferred_element_type=jnp.float32)
-            return c
-
-        return lax.fori_loop(0, width // kp, chunk, carry)
+                total[rows, c0 : c0 + kc] += jnp.dot(
+                    left, table, preferred_element_type=jnp.float32
+                )
+            return c
+
+        lax.fori_loop(0, width // kp, chunk, 0)
+
+    near_rows = pl.ds(pl.multiple_of(side * near_docs, near_docs), near_docs)
+
+    def project_near(s, carry):
+        @pl.when(s + ahead < steps)
+        def _():
+            send(s + ahead, 0)
+
+        def one(k, c):
+            near_copy(s, k).wait()
+            return c
+
+        lax.fori_loop(1, half, one, 0)
+        near_own(s).wait()
+        multiply(near.at[s], whole_ranks + place * near_steps + s, near_rows)
+        return carry
+
+    lax.fori_loop(0, near_steps, project_near, 0)
+
+    def project(s, carry):
+        @pl.when(s + ahead + near_steps < steps)
+        def _():
+            send(s + ahead + near_steps, 0)
+
+        def one(k, c):
+            grad_copy(s, k).wait()
+            return c
+
+        lax.fori_loop(1, nd, one, 0)
+        own_copy(s).wait()
+        multiply(landed.at[s], doc * steps + s, slice(None))
+        return carry
 
     lax.fori_loop(0, steps, project, 0)
 
@@ -212,7 +269,8 @@
     docs, tokens, width = activations.shape
     rank = adapter_down_matrix.shape[1]
     scale = 1.0 / math.sqrt(rank * width * nf * tokens)
-    steps = rank // nd
+    near_steps = rank // HALVED // (nd // 2)
+    steps = (rank - rank // HALVED) // nd
     rows_len, cols_len = PROJECTED_DIMS // nd, PROJECTED_DIMS // nf
     vmem = pl.BlockSpec(memory_space=pltpu.VMEM)
     bf16, f32 = jnp.bfloat16, jnp.float32
@@ -246,6 +304,7 @@
         out_specs=(vmem, vmem),
         scratch_shapes=[
             pltpu.VMEM((steps, docs * nd, width), bf16),
+            pltpu.VMEM((near_steps, docs * nd // 2, width), bf16),
             pltpu.VMEM((ROWS, PROJECTED_DIMS), jnp.int32),
             pltpu.VMEM((docs * nd, PROJECTED_DIMS), f32),
             pltpu.VMEM((targets.shape[0], PROJECTED_DIMS), bf16),
@@ -255,6 +314,7 @@
             pltpu.VMEM((nd, docs, cols_len), bf16),
             pltpu.VMEM((nf, docs * nd, cols_len), bf16),
             dma((steps, nd)), dma((steps, nd)), dma((steps,)),
+            dma((near_steps, nd // 2)), dma((near_steps, nd // 2)), dma((near_steps,)),
             dma((nd,)), dma((nd,)), dma((nf,)), dma((nf,)),
             dma((nd,)), dma((nd,)), dma((nd,)), dma((nd,)), dma((nf,)), dma((nf,)),
         ],

time: 303 us -> 255 us (0.84)
  Pallas kernels: 266 us -> 218 us
    pallas_call x1, Pallas kernels: 239 us -> 190 us  [body(): pl.pallas_call(functools.partial(project_kernel, nd, nf, scale), out_shap...]
where the time goes in v2:
time: 255 us; the launch traced here: 254 us
  Pallas kernels  218 us (85%)
  matrix products  19.7 us (8%)
  local copies, waits for them, and re-layouts  15.4 us (6%)
    pallas_call x1, Pallas kernels, body(): pl.pallas_call(functools.partial(project_kernel, nd, nf, scale), out_shap...  190 us
    pallas_call x1, Pallas kernels, body(): pl.pallas_call(functools.partial(rank_kernel, nf), out_shape=jax.ShapeDty...  27.6 us
    dot_general x1, matrix products, body(): jnp.einsum('esr,esc->rec', low.reshape(docs, tokens, rank), cotangents, p...  11.4 us
    dot_general x1, local copies, waits for them, and re-layouts, body(): jnp.einsum('esr,esc->rec', low.reshape(docs, tokens, rank), cotangents, p...  11.2 us
    dot_general x1, matrix products, body(): jnp.dot(activations.reshape(docs * tokens, width), adapter_down_matrix, p...  8.22 us

profile of v2, /device:TPU:1, one launch (start us, length us, event | category | flops | bytes accessed | tf_op | source)
XLA Modules:
  0.0 254.3 jit_solution(7614727323619603344)
XLA Ops:
  0.6 0.0 copy-start
  0.6 1.0 copy-done
  1.7 8.2 %convolution_convert_fusion.part_ref = bf16[4096,128]{1,0:T(8,128)(2,1)S(1)} fusion(bf16[4096,2048]{1,0:T(8,128)(2,1)} %bitcast.11, bf16[2048,128]{1,0:T(8,128)(2,1)S(1)} %copy-done), kind=kOutput, calls=%fused_computation.2 | convolution fusion | flops 2148007936 | bytes 18350080 | tf_op jit(solution)/shard_map/dot_general | solution.py:279
  9.9 27.6 %shard_map.68 = bf16[4096,128]{1,0:T(8,128)(2,1)S(1)} custom-call(bf16[4096,128]{1,0:T(8,128)(2,1)S(1)} %convolution_convert_fusion.part_ref), custom_call_target="tpu_custom_call" | custom-call | tf_op jit(solution)/shard_map/pallas_call | solution.py:282
  37.5 11.4 %fusion.1 = bf16[16,128,2048]{2,1,0:T(8,128)(2,1)} fusion(bf16[16,256,128]{2,1,0:T(8,128)(2,1)S(1)} %bitcast.9, bf16[16,256,2048]{2,1,0:T(8,128)(2,1)} %param.6), kind=kOutput, calls=%fused_computation.3 | convolution fusion | flops 2147483648 | bytes 26214400 | tf_op jit(solution)/shard_map/esr,esc->rec/dot_general | solution.py:292
  48.9 11.2 %copy.13 = bf16[16,128,2048]{2,0,1:T(8,128)(2,1)} copy(bf16[16,128,2048]{2,1,0:T(8,128)(2,1)} %fusion.1) | data formatting | bytes 16777216 | tf_op jit(solution)/shard_map/esr,esc->rec/dot_general | solution.py:292
  60.8 190.3 %shard_map.69 = (f32[256,512]{1,0:T(8,128)}, f32[16,128]{1,0:T(8,128)}) custom-call(s32[1]{0:T(128)S(6)} %copy.16.seed_ref, bf16[128,16,2048]{2,1,0:T(8,128)(2,1)} %bitcast.10, bf16[128,256]{1,0:T(8,128)(2,1)} %tin_ref.1), custom_call_target="tpu_custom_call" | custom-call | tf_op jit(solution)/shard_map/pallas_call | solution.py:295
  251.1 1.9 copy.17
  253.0 1.3 copy.18
Async XLA Ops:
  0.6 1.0 copy-start

commit v3 on v2

--- a/solution.py
+++ b/solution.py
@@ -81,6 +81,14 @@
         total += got[lax.rem(me + k, shards)].astype(jnp.float32)
     out_ref[block(me), :] = total.astype(jnp.bfloat16)
     run(exchange("fsdp", shards, lambda p: out_ref.at[block(me)], lambda m: out_ref.at[block(m)], s1, r1))
+
+
+def grads_kernel(low_ref, cot_ref, out_ref, held):
+    for e in range(low_ref.shape[0]):
+        held[:, e, :] = lax.dot_general(
+            low_ref[e], cot_ref[e], (((0,), (0,)), ((), ())), preferred_element_type=jnp.float32
+        )
+    out_ref[...] = held[...].astype(jnp.bfloat16)
 
 
 def project_kernel(
@@ -289,9 +297,19 @@
             collective_id=0, has_side_effects=True, vmem_limit_bytes=32 * 2**20
         ),
     )(part)
-    grads = jnp.einsum(
-        "esr,esc->rec", low.reshape(docs, tokens, rank), cotangents, preferred_element_type=f32
-    ).astype(bf16)
+    tile = min(512, width)
+    grads = pl.pallas_call(
+        grads_kernel,
+        grid=(width // tile,),
+        out_shape=jax.ShapeDtypeStruct((rank, docs, width), bf16),
+        in_specs=[
+            pl.BlockSpec((docs, tokens, rank), lambda j: (0, 0, 0)),
+            pl.BlockSpec((docs, tokens, tile), lambda j: (0, 0, j)),
+        ],
+        out_specs=pl.BlockSpec((rank, docs, tile), lambda j: (0, 0, j)),
+        scratch_shapes=[pltpu.VMEM((rank, docs, tile), f32)],
+        compiler_params=pltpu.CompilerParams(vmem_limit_bytes=40 * 2**20),
+    )(low.reshape(docs, tokens, rank), cotangents)
     return pl.pallas_call(
         functools.partial(project_kernel, nd, nf, scale),
         out_shape=(

time: 255 us -> 245 us (0.961)
  matrix products: 19.7 us -> 8.22 us
  Pallas kernels: 218 us -> 228 us
  local copies, waits for them, and re-layouts: 15.4 us -> 7.42 us
    dot_general x1 -> x0, matrix products: 11.4 us -> none  [body(): jnp.einsum('esr,esc->rec', low.reshape(docs, tokens, rank), cotangents, p...]
    dot_general x1 -> x0, local copies, waits for them, and re-layouts: 11.2 us -> none  [body(): jnp.einsum('esr,esc->rec', low.reshape(docs, tokens, rank), cotangents, p...]
    pallas_call x0 -> x1, Pallas kernels: none -> 10.3 us  [body(): pl.pallas_call(grads_kernel, grid=(width // tile,), out_shape=jax.ShapeDt...]
    unnamed x4 -> x6, local copies, waits for them, and re-layouts: 4.2 us -> 7.42 us
where the time goes in v3:
time: 245 us
  Pallas kernels  228 us (93%)
  matrix products  8.22 us (3%)
  local copies, waits for them, and re-layouts  7.42 us (3%)
    pallas_call x1, Pallas kernels, body(): pl.pallas_call(functools.partial(project_kernel, nd, nf, scale), out_shap...  190 us
    pallas_call x1, Pallas kernels, body(): pl.pallas_call(functools.partial(rank_kernel, nf), out_shape=jax.ShapeDty...  27.6 us
    pallas_call x1, Pallas kernels, body(): pl.pallas_call(grads_kernel, grid=(width // tile,), out_shape=jax.ShapeDt...  10.3 us
    dot_general x1, matrix products, body(): jnp.dot(activations.reshape(docs * tokens, width), adapter_down_matrix, p...  8.22 us
    unnamed x6, local copies, waits for them, and re-layouts  7.42 us

profile of v3, /device:TPU:1, one launch (start us, length us, event | category | flops | bytes accessed | tf_op | source)
XLA Modules:
  0.0 244.8 jit_solution(10063777404833267615)
XLA Ops:
  0.6 0.0 copy-start
  0.6 1.0 copy-done
  1.7 8.2 %convolution_convert_fusion.part_ref = bf16[4096,128]{1,0:T(8,128)(2,1)S(1)} fusion(bf16[4096,2048]{1,0:T(8,128)(2,1)} %bitcast.5, bf16[2048,128]{1,0:T(8,128)(2,1)S(1)} %copy-done), kind=kOutput, calls=%fused_computation | convolution fusion | flops 2148007936 | bytes 18350080 | tf_op jit(solution)/shard_map/dot_general | solution.py:287
  9.9 27.6 %shard_map.68 = bf16[4096,128]{1,0:T(8,128)(2,1)S(1)} custom-call(bf16[4096,128]{1,0:T(8,128)(2,1)S(1)} %convolution_convert_fusion.part_ref), custom_call_target="tpu_custom_call" | custom-call | tf_op jit(solution)/shard_map/pallas_call | solution.py:290
  37.5 10.3 %shard_map.69.grads_ref = bf16[128,16,2048]{2,1,0:T(8,128)(2,1)S(1)} custom-call(bf16[16,256,128]{2,1,0:T(8,128)(2,1)S(1)} %bitcast.4, bf16[16,256,2048]{2,1,0:T(8,128)(2,1)} %cot_ref.1), custom_call_target="tpu_custom_call" | custom-call | tf_op jit(solution)/shard_map/pallas_call | solution.py:301
  47.8 0.0 copy-start.1
  47.8 3.2 %copy-done.1 = bf16[128,16,2048]{2,1,0:T(8,128)(2,1)} copy-done((bf16[128,16,2048]{2,1,0:T(8,128)(2,1)}, bf16[128,16,2048]{2,1,0:T(8,128)(2,1)S(1)}, u32[]{:S(2)}) %copy-start.1) | copy-done | bytes 8388632
  51.6 190.0 %shard_map.70 = (f32[256,512]{1,0:T(8,128)}, f32[16,128]{1,0:T(8,128)}) custom-call(s32[1]{0:T(128)S(6)} %copy.9.seed_ref, bf16[128,16,2048]{2,1,0:T(8,128)(2,1)} %copy-done.1, bf16[128,256]{1,0:T(8,128)(2,1)} %tin_ref.1), custom_call_target="tpu_custom_call" | custom-call | tf_op jit(solution)/shard_map/pallas_call | solution.py:313
  241.7 1.9 copy.10
  243.5 1.3 copy.11
Async XLA Ops:
  0.6 1.0 copy-start
  47.8 3.2 %copy-start.1 = (bf16[128,16,2048]{2,1,0:T(8,128)(2,1)}, bf16[128,16,2048]{2,1,0:T(8,128)(2,1)S(1)}, u32[]{:S(2)}) copy-start(bf16[128,16,2048]{2,1,0:T(8,128)(2,1)S(1)} %shard_map.69.grads_ref) | copy-start | bytes 25165828
